TPU v7x, 256 devices: a whole 4x4x8 slice. The times are simulated.
256 devices in a mesh: store: 32 (over z, y), tp: 8 (over x, core).
Axes of the slice: x: 4, y: 4, z: 8, core: 2. Of those that a mesh axis runs over, the one named last changes fastest.
Arguments:
- query: bfloat16 [2560, 8192], P('store', 'tp')
- new_kv: bfloat16 [2, 2560, 1024], P(None, 'store', 'tp')
- kv_store: bfloat16 [2, 640, 512, 1024], P(None, 'store', None, 'tp'), may hold values from -6 to 6
- passage_ids: int32 [256, 10], P('store'), may hold values from 0 to 639, as said below
- residual_in: bfloat16 [2560, 8192], P('store', 'tp'), may hold values from -3 to 3
- out_weight: bfloat16 [8192, 8192], P('tp', 'store'), may hold values from -0.75 to 0.75
Outputs:
- layer_out: bfloat16 [2560, 8192], P('store', 'tp')
Inputs may be any that keep to these rules, and one draw needn't show every extreme that they name: `passage_ids`: store shard s holds passages s * 20 to (s + 1) * 20 - 1. In each aligned block of 8 rows (the queries of one index of store), every shard that is named at all is named exactly 5 times; popular shards are named in more blocks and low passage numbers within a shard are more popular.
All inputs are finite; a program needn't handle non-finite values.
Results may differ from a plain program's by a relative error of at most 0.018.
Values may be sent and summed in bfloat16 or wider, within the bound.
A program may use at most 64 MiB of HBM per device.

v0:
```python
import functools

import jax
import jax.numpy as jnp
import numpy as np
from jax import lax
from jax.experimental import pallas as pl
from jax.experimental.pallas import tpu as pltpu
from jax.sharding import PartitionSpec as P

HD = 128
PLEN = 512
GROUP = 8
SLOTS = 5
BLOCK = 16
WIDE = 3 * HD
PAD = 128
CHUNK = 16
Y_CHIPS = 4
TILES = (2, 0, 1)
MESH = pl.DeviceIdType.MESH
BF = jnp.bfloat16
F32 = jnp.float32
SCALE = 1.0 / HD**0.5
VMEM = pl.BlockSpec(memory_space=pltpu.VMEM)
HEADS = tuple(3 * g + b for b in TILES for g in range(3) if 3 * g + b < GROUP)
PIECES = GROUP
HBM = pl.BlockSpec(memory_space=pltpu.HBM)


def iota(shape, dim):
    return lax.broadcasted_iota(jnp.int32, shape, dim)


def dot(a, b):
    return jnp.dot(a, b, preferred_element_type=F32)


def row_parts(k):
    inner = jnp.bitwise_and(k, BLOCK - 1)
    group = (
        (inner >= SLOTS).astype(jnp.int32)
        + (inner >= 2 * SLOTS).astype(jnp.int32)
        + (inner >= 3 * SLOTS).astype(jnp.int32)
    )
    slot = jnp.right_shift(k, 4) * SLOTS + inner - SLOTS * group
    return slot, group


def as_row(column):
    return jnp.transpose(jnp.broadcast_to(column, (column.shape[0], HD)))[0:1, :]


def stream_slots(ids, pass_local):
    rows, width = ids.shape
    stream = iota((PAD, width), 0)
    spread = jnp.zeros((PAD, width), F32)
    place = jnp.full((PAD, width), -1, jnp.int32)
    for r in range(rows):
        inside = (stream >= r * width) & (stream < (r + 1) * width)
        spread = jnp.where(inside, ids[r : r + 1, :].astype(F32), spread)
        place = jnp.where(inside, stream - r * width, place)
    hit = place == iota((PAD, width), 1)
    passage = jnp.sum(jnp.where(hit, spread, 0.0), axis=1, keepdims=True)
    real = iota((PAD, 1), 0) < rows * width
    owner = jnp.floor((passage + 0.5) * (1.0 / pass_local))
    local = jnp.where(real, passage - owner * pass_local, 0.0)
    owner = jnp.where(real, owner, -1.0)
    same = owner == as_row(owner)
    earlier = iota((PAD, PAD), 1) < iota((PAD, PAD), 0)
    position = jnp.sum(jnp.where(same & earlier, 1.0, 0.0), axis=1, keepdims=True)
    return jnp.where(real, owner * SLOTS + position, -1.0), local


def remote(src, dst, send, recv, device):
    return pltpu.make_async_remote_copy(
        src_ref=src, dst_ref=dst, send_sem=send, recv_sem=recv, device_id=device, device_id_type=MESH
    )


def outward(k, stores):
    odd = jnp.bitwise_and(k, 1)
    return stores // 2 + jnp.where(odd == 1, lax.div(k, 2), -lax.div(k, 2))


def exchange_copy(k, me, tp, stores, msg, recv, send_sem, recv_sem):
    to = lax.rem(me + outward(k, stores), stores)
    return remote(
        msg.at[pl.ds(pl.multiple_of(to * BLOCK, BLOCK), BLOCK)],
        recv.at[pl.ds(pl.multiple_of(me * BLOCK, BLOCK), BLOCK)],
        send_sem.at[k],
        recv_sem.at[k],
        (to, tp),
    )


def pack(stores, slot, wide_ref, msg_ref):
    rows = stores * BLOCK
    row_slot, row_group = row_parts(iota((rows, 1), 0))
    wanted = jnp.where(row_group < 3, row_slot, -2).astype(F32)
    pick = jnp.where(wanted == as_row(slot), 1.0, 0.0).astype(BF)
    message = dot(pick, wide_ref[:, 2 * WIDE : 3 * WIDE])
    message = jnp.where(row_group == 1, dot(pick, wide_ref[:, WIDE : 2 * WIDE]), message)
    message = jnp.where(row_group == 0, dot(pick, wide_ref[:, 0:WIDE]), message)
    msg_ref[...] = message.astype(BF)


def sort_slots(n_chunks, pass_local, recv_ref, lower_ref, sorted_ref):
    rows = recv_ref.shape[0]
    places = sorted_ref.shape[0]
    _, group = row_parts(iota((rows, 1), 0))
    passage = recv_ref[:, 2 * HD : 3 * HD].astype(F32)
    lane = iota((rows, HD), 1).astype(F32)
    member = jnp.where((group == 2) & (passage == lane), 1.0, 0.0)
    rank = dot(lower_ref[...], member.astype(BF))
    counts = jnp.sum(member, axis=0, keepdims=True)
    chunks = jnp.floor((counts + (CHUNK - 1)) * (1.0 / CHUNK))
    upto = jnp.where(iota((HD, HD), 0) <= iota((HD, HD), 1), 1.0, 0.0).astype(BF)
    ends = dot(jnp.broadcast_to(chunks, (8, HD)).astype(BF), upto)[0:1, :]
    firsts = ends - chunks
    place = jnp.sum(member * (rank + CHUNK * firsts), axis=1, keepdims=True)
    one = pltpu.roll(jnp.broadcast_to(place, (rows, HD)), rows - SLOTS, 0)
    two = pltpu.roll(jnp.broadcast_to(place, (rows, HD)), rows - 2 * SLOTS, 0)
    place = jnp.where(group == 0, two, jnp.where(group == 1, one, place))
    place = jnp.where(group < 3, place, -1.0)
    place_row = jnp.transpose(place)[0:1, :]
    _, group_row = row_parts(iota((1, rows), 1))
    target = iota((places, 1), 0).astype(F32)
    for g in range(3):
        pick = jnp.where(target == jnp.where(group_row == g, place_row, -2.0), 1.0, 0.0).astype(BF)
        sorted_ref[:, g * WIDE : (g + 1) * WIDE] = dot(pick, recv_ref[...]).astype(BF)
    return place, jnp.where(iota((1, HD), 1) < pass_local, ends, 1e9)


def attend_chunks(n_chunks, pass_local, limits, sorted_ref, kv_ref, result_ref):
    lanes = iota((CHUNK, HD), 1)
    head_lane = jnp.bitwise_and(lanes, GROUP - 1)
    across = (((1,), (1,)), ((), ()))
    down = (((0,), (0,)), ((), ()))

    def attend(c, carry):
        index = jnp.sum(jnp.where(limits <= c.astype(F32), 1.0, 0.0)).astype(jnp.int32)
        index = jnp.clip(index, 0, pass_local - 1)
        at = pl.ds(pl.multiple_of(c * CHUNK, CHUNK), CHUNK)
        queries = jnp.concatenate(
            [sorted_ref[at, h * HD : (h + 1) * HD] for h in range(GROUP)], axis=0
        )
        scores = lax.dot_general(kv_ref[0, index], queries, across, preferred_element_type=F32)
        highest = jnp.max(scores, axis=0, keepdims=True)
        terms = jnp.exp2((scores - highest) * (SCALE * 1.4426950408889634))
        total = jnp.sum(terms, axis=0, keepdims=True)
        mixed = lax.dot_general(
            kv_ref[1, index], terms.astype(BF), down, preferred_element_type=F32
        )
        mixed = jnp.transpose(mixed * (1.0 / total))
        lse = highest * SCALE + jnp.log(total)
        lse = jnp.transpose(jnp.broadcast_to(lse, (8, GROUP * CHUNK)))[:, 0:1]
        sums = jnp.zeros((CHUNK, HD), F32)
        for h in range(GROUP):
            part = slice(h * CHUNK, (h + 1) * CHUNK)
            result_ref[at, h * HD : (h + 1) * HD] = mixed[part].astype(BF)
            sums = jnp.where(head_lane == h, lse[part], sums)
        high = sums.astype(BF).astype(F32)
        middle = (sums - high).astype(BF).astype(F32)
        low = sums - high - middle
        sums = jnp.where(lanes < GROUP, high, jnp.where(lanes < 2 * GROUP, middle, low))
        result_ref[at, GROUP * HD :] = sums.astype(BF)
        return carry

    lax.fori_loop(0, n_chunks, attend, 0, unroll=14)


def unsort(home, group, tile, result_ref, back_ref):
    back = dot(home, result_ref[:, (6 + tile) * HD : (7 + tile) * HD])
    back = jnp.where(group == 1, dot(home, result_ref[:, (3 + tile) * HD : (4 + tile) * HD]), back)
    back = jnp.where(group == 0, dot(home, result_ref[:, tile * HD : (tile + 1) * HD]), back)
    back_ref[tile] = back.astype(BF)


def kernel(
    stores,
    tps,
    y_chips,
    pass_local,
    n_chunks,
    q_hbm,
    new_hbm,
    kv_hbm,
    id_hbm,
    res_hbm,
    w_hbm,
    out_ref,
    q_ref,
    new_ref,
    kv_ref,
    id_ref,
    res_ref,
    wide,
    msg,
    recv,
    lower,
    sorted_ref,
    result,
    back,
    home,
    block,
    weight,
    part,
    pair,
    both,
    others,
    total,
    final,
    load_sem,
    go_send,
    go_recv,
    ex_send,
    ex_recv,
    w_send,
    w_recv,
    right_send,
    right_recv,
    left_send,
    left_recv,
    pair_send,
    pair_recv,
    sum_send,
    sum_recv,
    end_send,
    end_recv,
):
    me, tp = lax.axis_index("store"), lax.axis_index("tp")
    zs = stores // y_chips
    z = lax.div(me, y_chips)
    y = me - z * y_chips
    streams, width = q_ref.shape
    w_cols = w_hbm.shape[1]
    cut = width // tps
    diagonal = z == tp
    barrier = pltpu.get_barrier_semaphore()

    def greet(device):
        pl.semaphore_signal(barrier, inc=1, device_id=device, device_id_type=MESH)

    def greet_store(k, carry):
        greet((lax.rem(me + outward(k, stores), stores), tp))
        return carry

    lax.fori_loop(1, stores, greet_store, 0)
    for k in range(1, tps):
        greet((me, lax.rem(tp + k, tps)))
    for other in range(tps):

        @pl.when(jnp.logical_not(diagonal & (tp == other)))
        def _():
            greet((tp * y_chips + y, other))

    loads = [
        pltpu.make_async_copy(src, dst, load_sem.at[i])
        for i, (src, dst) in enumerate(
            [
                (id_hbm, id_ref),
                (q_hbm, q_ref),
                (kv_hbm, kv_ref),
                (new_hbm, new_ref),
                (res_hbm, res_ref),
                (w_hbm, weight.at[y]),
            ]
        )
    ]
    for load in loads:
        load.start()

    loads[0].wait()
    slot, local = stream_slots(id_ref[...], pass_local)
    wide[streams:, 0:width] = jnp.zeros((PAD - streams, width), BF)
    wide[:, width:] = jnp.broadcast_to(local, (PAD, HD)).astype(BF)
    loads[1].wait()
    wide[0:streams, 0:width] = q_ref[...]
    pack(stores, slot, wide, msg)
    pl.semaphore_wait(barrier, stores + 2 * tps - 2 - diagonal.astype(jnp.int32))

    def go(k, carry):
        exchange_copy(k, me, tp, stores, msg, recv, go_send, go_recv).start()
        return carry

    def went(k, carry):
        exchange_copy(k, me, tp, stores, msg, recv, go_send, go_recv).wait()
        return carry

    lax.fori_loop(1, stores, go, 0)
    above = (z * y_chips + lax.rem(y + 1, y_chips), tp)
    below = (z * y_chips + lax.rem(y + y_chips - 1, y_chips), tp)
    middle = w_hbm.shape[0] // 2

    def weight_up(came):
        return remote(
            w_hbm,
            weight.at[lax.rem(y + y_chips - 1, y_chips) if came else y],
            w_send.at[0],
            w_recv.at[0],
            above,
        )

    def weight_down(came):
        return remote(
            w_hbm,
            weight.at[lax.rem(y + 1, y_chips) if came else y],
            w_send.at[1],
            w_recv.at[1],
            below,
        )

    def half_up(came):
        at = weight.at[lax.rem(y + y_chips - (2 if came else 1), y_chips), 0:middle]
        return remote(at, at, w_send.at[2], w_recv.at[2], above)

    def half_down(came):
        at = weight.at[lax.rem(y + (2 if came else 1), y_chips), middle:]
        return remote(at, at, w_send.at[3], w_recv.at[3], below)

    near = [weight_up, weight_down][: y_chips - 1]
    far = [half_up, half_down] if y_chips > 3 else []
    for copy in near:
        copy(False).start()

    mine = pl.ds(pl.multiple_of(me * BLOCK, BLOCK), BLOCK)
    recv[mine, :] = msg[mine, :]
    rows = stores * BLOCK
    lower[...] = jnp.where(iota((rows, rows), 1) < iota((rows, rows), 0), 1.0, 0.0).astype(BF)
    result[n_chunks * CHUNK :, :] = jnp.zeros(
        (result.shape[0] - n_chunks * CHUNK, result.shape[1]), BF
    )
    loads[3].wait()
    new_key = new_ref[0].astype(F32)
    new_value = new_ref[1].astype(F32)
    own = [
        jnp.sum(q_ref[:, h * HD : (h + 1) * HD].astype(F32) * new_key, axis=1, keepdims=True)
        * SCALE
        for h in range(GROUP)
    ]
    loads[2].wait()
    lax.fori_loop(1, stores, went, 0)

    place, limits = sort_slots(n_chunks, pass_local, recv, lower, sorted_ref)
    attend_chunks(n_chunks, pass_local, limits, sorted_ref, kv_ref, result)
    for copy in near:
        copy(True).wait_recv()
    for copy in far:
        copy(False).start()
    places = result.shape[0]
    spread = jnp.broadcast_to(place[:, 0:1], (rows, places))
    send_home = jnp.where(spread == iota((rows, places), 1).astype(F32), 1.0, 0.0).astype(BF)
    _, group = row_parts(iota((rows, 1), 0))

    def give(tile, k, carry):
        exchange_copy(
            k, me, tp, stores, back.at[tile], home.at[tile], ex_send.at[tile], ex_recv.at[tile]
        ).start()
        return carry

    def given(tile, k, carry):
        exchange_copy(
            k, me, tp, stores, back.at[tile], home.at[tile], ex_send.at[tile], ex_recv.at[tile]
        ).wait()
        return carry

    for tile in TILES:
        unsort(send_home, group, tile, result, back)
        lax.fori_loop(1, stores, functools.partial(give, tile), 0)
        home[tile, mine, :] = back[tile, mine, :]
    row_slot, row_group = row_parts(iota((1, rows), 1))
    match = slot[0:streams] == row_slot.astype(F32)
    picks = [jnp.where(match & (row_group == g), 1.0, 0.0).astype(BF) for g in range(3)]

    half = zs // 2
    to_right = (lax.rem(z + 1, zs) * y_chips + y, tp)
    to_left = (lax.rem(z + zs - 1, zs) * y_chips + y, tp)

    def on_right(k, c):
        return k < half or (k == half and c < PIECES // 2)

    def on_left(k, c):
        return k < half or (k == half and c >= PIECES // 2)

    def right(k, c, came):
        at = block.at[lax.rem(z + zs - (k if came else k - 1), zs), c]
        return remote(at, at, right_send.at[k - 1, c], right_recv.at[k - 1, c], to_right)

    def left(k, c, came):
        at = block.at[lax.rem(z + (k if came else k - 1), zs), c]
        return remote(at, at, left_send.at[k - 1, c], left_recv.at[k - 1, c], to_left)

    def pass_on(k, c):
        if on_right(k, c):
            right(k, c, False).start()
        if on_left(k, c):
            left(k, c, False).start()

    for tile in TILES:
        lax.fori_loop(1, stores, functools.partial(given, tile), 0)
        if tile == 2:
            sums = dot(picks[2], home[tile])
        for h in range(tile, GROUP, 3):
            lse = sums[:, h : h + 1] + sums[:, GROUP + h : GROUP + h + 1]
            lse = lse + sums[:, 2 * GROUP + h : 2 * GROUP + h + 1]
            highest = jnp.maximum(lse, own[h])
            first = jnp.exp(lse - highest)
            second = jnp.exp(own[h] - highest)
            mixed = dot(picks[h // 3], home[tile]) * first + new_value * second
            piece = HEADS.index(h)
            block[z, piece] = (mixed * (1.0 / (first + second))).astype(BF)
            pass_on(1, piece)

    xs = tps // 2
    x = lax.div(tp, 2)
    core = tp - 2 * x

    def pair_copy(i):
        return remote(
            part.at[i, 1 - core], pair.at[i], pair_send.at[i], pair_recv.at[i], (me, 2 * x + 1 - core)
        )

    def sum_copy(i, k):
        to = lax.rem(x + k, xs)
        return remote(
            both.at[i, to], others.at[i, x], sum_send.at[i, k], sum_recv.at[i, k], (me, 2 * to + core)
        )

    def multiply(i):
        for v in range(y_chips):
            product = sum(
                dot(block[where[i], piece], weight[v, h * HD : (h + 1) * HD, :])
                for piece, h in enumerate(HEADS)
            )
            for u in range(w_cols // cut):
                column = v * (w_cols // cut) + u
                part[i, column % 2, column // 2] = product[:, u * cut : (u + 1) * cut].astype(BF)
        pair_copy(i).start()

    def across(i):
        pair_copy(i).wait_recv()
        both[i] = (part[i, core].astype(F32) + pair[i].astype(F32)).astype(BF)
        for k in range(1, xs):
            sum_copy(i, k).start()

    def end_copy(i):
        return remote(
            total.at[i],
            final.at[tp],
            end_send.at[i],
            end_recv.at[tp],
            (where[i] * y_chips + y, z),
        )

    def add_up(i):
        value = part[i, core, x].astype(F32)
        for k in range(1, xs):
            sum_copy(i, k).wait_recv()
        value = value + pair[i, x].astype(F32)
        for k in range(1, xs):
            value = value + others[i, lax.rem(x + xs - k, xs)].astype(F32)
        total[i] = value.astype(BF)
        if i == 0:

            @pl.when(diagonal)
            def _():
                final[tp] = total[i]

            @pl.when(jnp.logical_not(diagonal))
            def _():
                end_copy(i).start()

        else:
            end_copy(i).start()

    offsets = [0]
    for k in range(1, half):
        offsets += [-k, k]
    offsets.append(-half)
    where = [lax.rem(z + zs + o, zs) for o in offsets]
    loads[5].wait()
    for copy in far:
        copy(True).wait_recv()
    ready = [[0]] + [[2 * k - 1, 2 * k] for k in range(1, half)] + [[zs - 1]]
    for k in range(1, half + 1):
        tasks = [
            [functools.partial(step, i) for i in (ready[k - lag] if k >= lag else [])]
            for lag, step in ((1, multiply), (2, across), (3, add_up))
        ]
        for c in range(PIECES):
            if on_right(k, c):
                right(k, c, True).wait_recv()
                if on_right(k + 1, c):
                    right(k + 1, c, False).start()
            if on_left(k, c):
                left(k, c, True).wait_recv()
                if on_left(k + 1, c):
                    left(k + 1, c, False).start()
            if c < len(tasks):
                for task in tasks[c]:
                    task()
    for i in ready[half - 1]:
        across(i)
    multiply(zs - 1)
    for i in ready[half]:
        across(i)
    for blocks in ready[max(half - 2, 0) :]:
        for i in blocks:
            add_up(i)

    loads[4].wait()
    for other in range(tps):

        @pl.when(jnp.logical_not(diagonal & (tp == other)))
        def _():
            remote(
                total.at[0], final.at[other], end_send.at[0], end_recv.at[other], (me, tp)
            ).wait_recv()

        at = slice(other * cut, (other + 1) * cut)
        out_ref[:, at] = (res_ref[:, at].astype(F32) + final[other].astype(F32)).astype(BF)

    for copy in near + far:
        copy(False).wait_send()
    for k in range(1, half + 1):
        for c in range(PIECES):
            if on_right(k, c):
                right(k, c, False).wait_send()
            if on_left(k, c):
                left(k, c, False).wait_send()
    for i in range(zs):
        pair_copy(i).wait_send()
        for k in range(1, xs):
            sum_copy(i, k).wait_send()
        if i == 0:

            @pl.when(jnp.logical_not(diagonal))
            def _():
                end_copy(i).wait_send()

        else:
            end_copy(i).wait_send()


def shards(y_chips, query, new_kv, kv_store, passage_ids, residual_in, out_weight):
    stores, tps = lax.axis_size("store"), lax.axis_size("tp")
    zs = stores // y_chips
    streams, width = query.shape
    pass_local = kv_store.shape[1]
    rows = stores * BLOCK
    n_chunks = (stores * SLOTS + pass_local * (CHUNK - 1)) // CHUNK
    places = -(-n_chunks * CHUNK // HD) * HD
    cut = width // tps
    dma = pltpu.SemaphoreType.DMA

    def vmem(*shape):
        return pltpu.VMEM(shape, BF)

    return pl.pallas_call(
        functools.partial(kernel, stores, tps, y_chips, pass_local, n_chunks),
        out_shape=pltpu.VMEM((streams, width), BF),
        in_specs=[HBM] * 6,
        out_specs=VMEM,
        scratch_shapes=[
            vmem(streams, width),
            vmem(*new_kv.shape),
            vmem(*kv_store.shape),
            pltpu.VMEM(passage_ids.shape, jnp.int32),
            vmem(streams, width),
            vmem(PAD, 3 * WIDE),
            vmem(rows, WIDE),
            vmem(rows, WIDE),
            vmem(rows, rows),
            vmem(places, 3 * WIDE),
            vmem(places, 3 * WIDE),
            vmem(3, rows, HD),
            vmem(3, rows, HD),
            vmem(zs, PIECES, streams, width // PIECES),
            vmem(y_chips, *out_weight.shape),
            vmem(zs, 2, tps // 2, streams, cut),
            vmem(zs, tps // 2, streams, cut),
            vmem(zs, tps // 2, streams, cut),
            vmem(zs, tps // 2, streams, cut),
            vmem(zs, streams, cut),
            vmem(tps, streams, cut),
            dma((6,)),
            dma((stores,)),
            dma((stores,)),
            dma((3, stores)),
            dma((3, stores)),
            dma((4,)),
            dma((4,)),
            dma((zs // 2, PIECES)),
            dma((zs // 2, PIECES)),
            dma((zs // 2, PIECES)),
            dma((zs // 2, PIECES)),
            dma((zs,)),
            dma((zs,)),
            dma((zs, tps // 2)),
            dma((zs, tps // 2)),
            dma((zs,)),
            dma((tps,)),
        ],
        compiler_params=pltpu.CompilerParams(
            collective_id=0, has_side_effects=True, vmem_limit_bytes=48 * 2**20
        ),
        name="decode",
    )(*[pltpu.with_memory_space_constraint(a, pltpu.HBM) for a in (query, new_kv, kv_store, passage_ids, residual_in, out_weight)])


def solution(mesh, y_chips=Y_CHIPS):
    placed = (
        P("store", "tp"),
        P(None, "store", "tp"),
        P(None, "store", None, "tp"),
        P("store", None),
        P("store", "tp"),
        P("tp", "store"),
    )
    return jax.shard_map(
        functools.partial(shards, y_chips),
        mesh=mesh,
        in_specs=placed,
        out_specs=P("store", "tp"),
        check_vma=False,
    )
```

profile of v0, /device:TPU:4, one launch (start us, length us, event | category | flops | bytes accessed | tf_op | source)
XLA Modules:
  0.0 72.2 jit_solution(15574031627052654191)
XLA Ops:
  0.0 71.6 %decode.1 = bf16[80,1024]{1,0:T(8,128)(2,1)S(1)} custom-call(bf16[80,1024]{1,0:T(8,128)(2,1)} %q_hbm.1, bf16[2,80,128]{2,1,0:T(8,128)(2,1)} %new_hbm.1, bf16[2,20,512,128]{3,2,1,0:T(8,128)(2,1)} %kv_hbm.1, s32[8,10]{1,0:T(8,128)} %id_hbm.1, bf16[80,1024]{1,0:T(8,128)(2,1)} %res_hbm.1, bf16[1024,256]{1,0:T(8,128)(2,1)} %w_hbm.1), custom_call_target="tpu_custom_call" | custom-call | tf_op jit(solution)/shard_map/decode/pallas_call | solution.py:560
  71.6 0.7 copy.8
where the time goes:
time: 72.7 us; the launch traced here: 72.2 us
  Pallas kernels  71.6 us (98%)
    pallas_call x1, Pallas kernels, shards(): pl.pallas_call(functools.partial(kernel, stores, tps, y_chips, pass_local...  71.6 us

commit v1 on v0

--- a/solution.py
+++ b/solution.py
@@ -427,16 +427,24 @@
             both.at[i, to], others.at[i, x], sum_send.at[i, k], sum_recv.at[i, k], (me, 2 * to + core)
         )
 
-    def multiply(i):
+    def multiply(blocks):
+        pieces = [
+            jnp.concatenate([block[where[i], piece] for i in blocks], axis=0)
+            for piece in range(PIECES)
+        ]
         for v in range(y_chips):
             product = sum(
-                dot(block[where[i], piece], weight[v, h * HD : (h + 1) * HD, :])
+                dot(pieces[piece], weight[v, h * HD : (h + 1) * HD, :])
                 for piece, h in enumerate(HEADS)
             )
-            for u in range(w_cols // cut):
-                column = v * (w_cols // cut) + u
-                part[i, column % 2, column // 2] = product[:, u * cut : (u + 1) * cut].astype(BF)
-        pair_copy(i).start()
+            for n, i in enumerate(blocks):
+                for u in range(w_cols // cut):
+                    column = v * (w_cols // cut) + u
+                    part[i, column % 2, column // 2] = product[
+                        n * streams : (n + 1) * streams, u * cut : (u + 1) * cut
+                    ].astype(BF)
+        for i in blocks:
+            pair_copy(i).start()
 
     def across(i):
         pair_copy(i).wait_recv()
@@ -484,10 +492,11 @@
         copy(True).wait_recv()
     ready = [[0]] + [[2 * k - 1, 2 * k] for k in range(1, half)] + [[zs - 1]]
     for k in range(1, half + 1):
-        tasks = [
-            [functools.partial(step, i) for i in (ready[k - lag] if k >= lag else [])]
-            for lag, step in ((1, multiply), (2, across), (3, add_up))
-        ]
+        tasks = [functools.partial(multiply, ready[k - 1])]
+        if k >= 2:
+            tasks += [functools.partial(across, i) for i in ready[k - 2]]
+        if k >= 3:
+            tasks += [functools.partial(add_up, i) for i in ready[k - 3]]
         for c in range(PIECES):
             if on_right(k, c):
                 right(k, c, True).wait_recv()
@@ -498,11 +507,10 @@
                 if on_left(k + 1, c):
                     left(k + 1, c, False).start()
             if c < len(tasks):
-                for task in tasks[c]:
-                    task()
+                tasks[c]()
     for i in ready[half - 1]:
         across(i)
-    multiply(zs - 1)
+    multiply(ready[half])
     for i in ready[half]:
         across(i)
     for blocks in ready[max(half - 2, 0) :]:

time: 72.7 us -> 72.3 us (level)
  no operation moved by 1% of the time
where the time goes in v1:
time: 72.3 us; the launch traced here: 72.2 us
  Pallas kernels  71.5 us (99%)
    pallas_call x1, Pallas kernels, shards(): pl.pallas_call(functools.partial(kernel, stores, tps, y_chips, pass_local...  71.5 us

profile of v1, /device:TPU:4, one launch (start us, length us, event | category | flops | bytes accessed | tf_op | source)
XLA Modules:
  0.0 72.2 jit_solution(611879098483125151)
XLA Ops:
  0.0 71.5 %decode.1 = bf16[80,1024]{1,0:T(8,128)(2,1)S(1)} custom-call(bf16[80,1024]{1,0:T(8,128)(2,1)} %q_hbm.1, bf16[2,80,128]{2,1,0:T(8,128)(2,1)} %new_hbm.1, bf16[2,20,512,128]{3,2,1,0:T(8,128)(2,1)} %kv_hbm.1, s32[8,10]{1,0:T(8,128)} %id_hbm.1, bf16[80,1024]{1,0:T(8,128)(2,1)} %res_hbm.1, bf16[1024,256]{1,0:T(8,128)(2,1)} %w_hbm.1), custom_call_target="tpu_custom_call" | custom-call | tf_op jit(solution)/shard_map/decode/pallas_call | solution.py:568
  71.5 0.7 copy.8

commit v2 on v1

--- a/solution.py
+++ b/solution.py
@@ -167,7 +167,7 @@
         result_ref[at, GROUP * HD :] = sums.astype(BF)
         return carry
 
-    lax.fori_loop(0, n_chunks, attend, 0, unroll=14)
+    lax.fori_loop(0, n_chunks, attend, 0, unroll=28)
 
 
 def unsort(home, group, tile, result_ref, back_ref):
@@ -378,10 +378,10 @@
     to_left = (lax.rem(z + zs - 1, zs) * y_chips + y, tp)
 
     def on_right(k, c):
-        return k < half or (k == half and c < PIECES // 2)
+        return k < half or (k == half and c % 2 == 0)
 
     def on_left(k, c):
-        return k < half or (k == half and c >= PIECES // 2)
+        return k < half or (k == half and c % 2 == 1)
 
     def right(k, c, came):
         at = block.at[lax.rem(z + zs - (k if came else k - 1), zs), c]

time: 72.3 us -> 72.2 us (level)
  no operation moved by 1% of the time
where the time goes in v2:
time: 72.2 us; the launch traced here: 72.1 us
  Pallas kernels  71.5 us (99%)
    pallas_call x1, Pallas kernels, shards(): pl.pallas_call(functools.partial(kernel, stores, tps, y_chips, pass_local...  71.5 us

profile of v2, /device:TPU:4, one launch (start us, length us, event | category | flops | bytes accessed | tf_op | source)
XLA Modules:
  0.0 72.1 jit_solution(11843667942005261642)
XLA Ops:
  0.0 71.5 %decode.1 = bf16[80,1024]{1,0:T(8,128)(2,1)S(1)} custom-call(bf16[80,1024]{1,0:T(8,128)(2,1)} %q_hbm.1, bf16[2,80,128]{2,1,0:T(8,128)(2,1)} %new_hbm.1, bf16[2,20,512,128]{3,2,1,0:T(8,128)(2,1)} %kv_hbm.1, s32[8,10]{1,0:T(8,128)} %id_hbm.1, bf16[80,1024]{1,0:T(8,128)(2,1)} %res_hbm.1, bf16[1024,256]{1,0:T(8,128)(2,1)} %w_hbm.1), custom_call_target="tpu_custom_call" | custom-call | tf_op jit(solution)/shard_map/decode/pallas_call | solution.py:568
  71.5 0.7 copy.8
